TPU v7x, 128 devices: a whole 4x4x4 slice. The times are simulated.
128 devices in a mesh: tm: 8 (over y, core), rows: 16 (over z, x).
Axes of the slice: x: 4, y: 4, z: 4, core: 2. Of those that a mesh axis runs over, the one named last changes fastest.
Arguments:
- video: bfloat16 [32, 128, 256, 128], P('tm', 'rows'), may hold values from -15 to 15
- clip_lengths: int32 [8], replicated, may hold values from 1 to 9, 32 in all
- norm_gain: float32 [128], replicated, may hold values from 0.5 to 1.5
- norm_shift: float32 [128], replicated, may hold values from -3 to 3
- conv_weight: bfloat16 [3, 3, 3, 128, 128], replicated, may hold values from -0.109375 to 0.109375
- conv_bias: float32 [128], replicated, may hold values from -3 to 3
- down_weight: bfloat16 [3, 3, 3, 128, 128], replicated, may hold values from -0.109375 to 0.109375
- down_bias: float32 [128], replicated, may hold values from -3 to 3
Outputs:
- encoded: bfloat16 [32, 64, 128, 128], P('tm', 'rows')
Inputs may be any that keep to these rules, and one draw needn't show every extreme that they name: `clip_lengths`: the lengths sum to 32; the longest clip has exactly 9 frames.
All inputs are finite; a program needn't handle non-finite values.
Results may differ from a plain program's by a relative error of at most 0.0051.
Values may be sent and summed in bfloat16 or wider, within the bound.
A program may use at most 192 MiB of HBM per device.

v0:
```python
import jax
import jax.numpy as jnp
from jax import lax
from jax.sharding import PartitionSpec as P

GROUPS = 32


EPSILON = 1e-06


def with_halo(cells, sides, width):
    for axis, dim in sides:
        count = lax.axis_size(axis)
        ends = count - 1
        head = lax.slice_in_dim(cells, 0, width, axis=dim)
        tail = lax.slice_in_dim(cells, cells.shape[dim] - width, cells.shape[dim], axis=dim)
        cells = jnp.concatenate(
            [
                lax.ppermute(tail, axis, [(i, (i + 1) % count) for i in range(ends)]),
                cells,
                lax.ppermute(head, axis, [((i + 1) % count, i) for i in range(ends)]),
            ],
            axis=dim,
        )
    return cells


def passed_along(value, axis, steps):
    count = lax.axis_size(axis)
    first, last = (max(0, -steps), min(count, count - steps))
    return lax.ppermute(value, axis, [(source, source + steps) for source in range(first, last)])


def clip_member(clip_lengths, frame_ids):
    clip_ends = jnp.cumsum(clip_lengths, dtype=jnp.int32)
    clip_starts = clip_ends - clip_lengths
    inside = (frame_ids[:, None] >= clip_starts[None, :]) & (
        frame_ids[:, None] < clip_ends[None, :]
    )
    return inside.astype(jnp.float32)


def clip_first_frame(clip_lengths, frame_ids):
    clip_ends = jnp.cumsum(clip_lengths, dtype=jnp.int32)
    clip_starts = clip_ends - clip_lengths
    inside = (frame_ids[:, None] >= clip_starts[None, :]) & (
        frame_ids[:, None] < clip_ends[None, :]
    )
    return jnp.sum(jnp.where(inside, clip_starts[None, :], 0), axis=1)


def margin(frame_block, at_top, bottom):
    padded = with_halo(frame_block, (("rows", 1),), 1)
    upper_rim = jnp.where(at_top, frame_block[:, :1], padded[:, :1])
    lower_rim = jnp.where(bottom, frame_block[:, -1:], padded[:, -1:])
    return jnp.concatenate([upper_rim, frame_block, lower_rim], axis=1)


def widen_columns(frame_block):
    columns = frame_block.shape[2]
    padded = jnp.pad(frame_block, ((0, 0), (0, 0), (1, 1), (0, 0)), mode="edge")
    return jnp.concatenate(
        [padded[:, :, col_tap : col_tap + columns] for col_tap in range(3)], axis=3
    )


def conv_taps(widened, sources, kernel, row_step, out_rows):
    running = None
    for time_tap in range(3):
        picked = jnp.take(widened, sources[:, time_tap], axis=0)
        for row_tap in range(3):
            sliced = lax.slice_in_dim(
                picked, row_tap, row_tap + row_step * (out_rows - 1) + 1, row_step, 1
            )
            term = jnp.einsum(
                "frwk,kc->frwc",
                sliced,
                kernel[time_tap, row_tap],
                preferred_element_type=jnp.float32,
            )
            running = term if running is None else running + term
    return running


def per_device(
    video, clip_lengths, norm_gain, norm_shift, conv_weight, conv_bias, down_weight, down_bias
):
    frames, band_rows, columns, channels = video.shape
    per_group = channels // GROUPS
    offset = lax.axis_index("tm") * frames
    at_top = lax.axis_index("rows") == 0
    bottom = lax.axis_index("rows") == lax.axis_size("rows") - 1
    height = band_rows * lax.axis_size("rows")
    conv_kernel = conv_weight.reshape(3, 3, 3 * channels, channels)
    down_kernel = down_weight.reshape(3, 3, 3 * channels, channels)
    time_lags = jnp.arange(3, dtype=jnp.int32)
    own_ids = offset + jnp.arange(frames, dtype=jnp.int32)
    member = clip_member(clip_lengths, own_ids)
    clip_first = clip_first_frame(clip_lengths, own_ids)
    values = video.reshape(frames, band_rows * columns, GROUPS, per_group).astype(jnp.float32)
    totals = jnp.sum(values, axis=(1, 3))
    squares = jnp.sum(values * values, axis=(1, 3))
    clip_sum = jnp.dot(member.T, totals, precision=lax.Precision.HIGHEST)
    clip_square = jnp.dot(member.T, squares, precision=lax.Precision.HIGHEST)
    clip_sum, clip_square = lax.psum((clip_sum, clip_square), ("tm", "rows"))
    counts = (clip_lengths * (height * columns * per_group)).astype(jnp.float32)[:, None]
    means = clip_sum / counts
    scales = lax.rsqrt(clip_square / counts - means * means + EPSILON)
    block_member = clip_member(clip_lengths, jnp.maximum(own_ids, 0))
    frame_mean = jnp.repeat(
        jnp.dot(block_member, means, precision=lax.Precision.HIGHEST), per_group, axis=1
    )
    frame_scale = jnp.repeat(
        jnp.dot(block_member, scales, precision=lax.Precision.HIGHEST), per_group, axis=1
    )
    normed = (video.astype(jnp.float32) - frame_mean[:, None, None, :]) * frame_scale[
        :, None, None, :
    ]
    normed = normed * norm_gain + norm_shift
    hidden = jax.nn.silu(normed).astype(jnp.bfloat16)
    earlier = passed_along(hidden[-2:], "tm", 1)
    extended = jnp.concatenate([earlier, hidden], axis=0)
    sources = jnp.maximum(own_ids[:, None] - 2 + time_lags[None, :], clip_first[:, None]) - (
        offset - 2
    )
    running = conv_taps(
        widen_columns(margin(extended, at_top, bottom)), sources, conv_kernel, 1, band_rows
    )
    summed = (running + conv_bias + video.astype(jnp.float32)).astype(jnp.bfloat16)
    prior_sums = passed_along(summed[-2:], "tm", 1)
    summed_ext = jnp.concatenate([prior_sums, summed], axis=0)
    upper_row = passed_along(summed_ext[:, -1:], "rows", 1)
    upper_row = jnp.where(at_top, summed_ext[:, :1], upper_row)
    stacked = jnp.concatenate([upper_row, summed_ext], axis=1)
    padded = jnp.pad(stacked, ((0, 0), (0, 0), (1, 0), (0, 0)), mode="edge")
    widened = jnp.concatenate(
        [padded[:, :, col_tap : col_tap + columns - 1 : 2] for col_tap in range(3)], axis=3
    )
    down_sources = jnp.maximum(own_ids[:, None] - 2 + time_lags[None, :], clip_first[:, None]) - (
        offset - 2
    )
    running = conv_taps(widened, down_sources, down_kernel, 2, band_rows // 2)
    return (running + down_bias).astype(jnp.bfloat16)


def solution(mesh):
    placed = (P("tm", "rows", None, None), P(), P(), P(), P(), P(), P(), P())
    return jax.shard_map(
        per_device,
        mesh=mesh,
        in_specs=placed,
        out_specs=P("tm", "rows", None, None),
        check_vma=False,
    )
```

profile of v0, /device:TPU:40, one launch (start us, length us, event | category | flops | bytes accessed | tf_op | source)
XLA Modules:
  0.0 341.7 jit_solution(10787127204030355865)
XLA Ops:
  4.6 65.2 %all-reduce = (f32[8,32]{1,0:T(8,128)S(1)}, f32[8,32]{1,0:T(8,128)S(1)}) all-reduce(f32[8,32]{1,0:T(8,128)S(1)} %fusion.100, f32[8,32]{1,0:T(8,128)S(1)} %fusion.99), channel_id=1, replica_groups=mesh['tm'=8,'rows'=16] {'tm','rows'}, use_global_device_ids=true, to_apply=%region_6.7 | all-reduce | flops 512 | bytes 4096 | tf_op jit(solution)/shard_map/psum | solution.py:106
  70.6 3.1 fusion.19
  75.8 14.2 %collective-permute-done = bf16[2,8,256,128]{3,2,1,0:T(8,128)(2,1)S(1)} collective-permute-done((bf16[2,8,256,128]{3,2,1,0:T(8,128)(2,1)S(1)}, bf16[2,8,256,128]{3,2,1,0:T(8,128)(2,1)S(1)}, u32[]{:S(2)}, u32[]{:S(2)}) %collective-permute-start) | collective-permute-done | bytes 1048608 | tf_op jit(solution)/shard_map/ppermute | solution.py:32
  90.0 4.9 %collective-permute-start.2 = (bf16[6,1,256,128]{3,2,1,0:T(8,128)(2,1)S(1)}, bf16[6,1,256,128]{3,2,1,0:T(8,128)(2,1)}, u32[]{:S(2)}, u32[]{:S(2)}) collective-permute-start(bf16[6,1,256,128]{3,2,1,0:T(8,128)(2,1)S(1)} %pad_maximum_fusion.10), channel_id=1, source_target_pairs={{1,0},{2,1},{3,2},{4,3},{5,4},{6,5},{7,6},{8,7},{9,8},{10,9},{11,1... | collective-permute-start | bytes 1179656 | tf_op jit(solution)/shard_map/ppermute | solution.py:22
  95.0 7.1 %collective-permute-done.2 = bf16[6,1,256,128]{3,2,1,0:T(8,128)(2,1)} collective-permute-done((bf16[6,1,256,128]{3,2,1,0:T(8,128)(2,1)S(1)}, bf16[6,1,256,128]{3,2,1,0:T(8,128)(2,1)}, u32[]{:S(2)}, u32[]{:S(2)}) %collective-permute-start.2) | collective-permute-done | bytes 393248 | tf_op jit(solution)/shard_map/ppermute | solution.py:22
  107.4 10.3 %collective-permute-done.1 = bf16[6,1,256,128]{3,2,1,0:T(8,128)(2,1)} collective-permute-done((bf16[6,1,256,128]{3,2,1,0:T(8,128)(2,1)}, bf16[6,1,256,128]{3,2,1,0:T(8,128)(2,1)}, u32[]{:S(2)}, u32[]{:S(2)}) %collective-permute-start.1) | collective-permute-done | bytes 393248 | tf_op jit(solution)/shard_map/ppermute | solution.py:20
  118.8 7.1 %fusion.24 = (bf16[6,10,256,128]{3,2,1,0:T(8,128)(2,1)S(1)}, bf16[6,10,256,128]{3,2,1,0:T(8,128)(2,1)S(1)}) fusion(bf16[6,1,256,128]{3,2,1,0:T(8,128)(2,1)S(1)} %broadcast_select_fusion.7, bf16[2,8,256,128]{3,2,1,0:T(8,128)(2,1)S(1)} %collective-permute-done, bf16[4,8,256,128]{3,2,1,0:T(8,128)(2,1)S(1)} %fusion.19, ...), kind=kLoop, calls=%fused_computation.42 | loop fusion | flops 86507520 | bytes 11796480 | tf_op jit(solution)/shard_map/jit(_pad)/concatenate | solution.py:62
  125.9 6.6 %pad_maximum_fusion = bf16[6,10,256,384]{3,2,1,0:T(8,128)(2,1)} fusion(bf16[6,10,256,128]{3,2,1,0:T(8,128)(2,1)S(1)} %get-tuple-element.22, bf16[6,1,256,128]{3,2,1,0:T(8,128)(2,1)S(1)} %get-tuple-element.19, bf16[4,8,256,128]{3,2,1,0:T(8,128)(2,1)S(1)} %fusion.19, bf16[2,8,256,128]{3,2,1,0:T(8,128)(2,1)S(1)} %collective-permute-done, ...), kind=kLoop, calls=%fused_computation.6 | loop fusion | flops 70778880 | bytes 23592960 | tf_op jit(solution)/shard_map/concatenate | solution.py:63
  132.6 9.2 %gather_fusion.1 = bf16[4,10,256,384]{3,2,1,0:T(8,128)(2,1)} fusion(bf16[6,10,256,384]{3,2,1,0:T(8,128)(2,1)} %pad_maximum_fusion, s32[1024]{0:T(1024)S(1)} %pad_clamp_fusion.1), kind=kCustom, calls=%fused_computation.2.clone | custom fusion | bytes 15728656 | tf_op jit(solution)/shard_map/jit(_take)/gather | solution.py:71
  141.8 6.8 %fusion.83 = f32[4,8,256,128]{3,2,1,0:T(8,128)} fusion(bf16[3,3,384,128]{3,2,1,0:T(8,128)(2,1)S(1)} %bitcast.153, bf16[4,10,256,384]{3,2,1,0:T(8,128)(2,1)} %gather_fusion.1, pred[4]{0:T(512)(128)(4,1)S(1)} %copy-done.13), kind=kOutput, calls=%fused_computation.109 | convolution fusion | flops 809238528 | bytes 12157440 | tf_op jit(solution)/shard_map/frwk,kc->frwc/dot_general | solution.py:76
  148.6 3.9 %fusion.84 = f32[4,8,256,128]{3,2,1,0:T(8,128)} fusion(bf16[3,3,384,128]{3,2,1,0:T(8,128)(2,1)S(1)} %bitcast.154, bf16[4,10,256,384]{3,2,1,0:T(8,128)(2,1)S(1)} %copy-done.1, pred[4]{0:T(512)(128)(4,1)S(1)} %copy-done.13), kind=kOutput, calls=%fused_computation.111 | convolution fusion | flops 809238528 | bytes 12157440 | tf_op jit(solution)/shard_map/frwk,kc->frwc/dot_general | solution.py:76
  152.6 3.9 %fusion.85 = f32[4,8,256,128]{3,2,1,0:T(8,128)} fusion(bf16[3,3,384,128]{3,2,1,0:T(8,128)(2,1)S(1)} %bitcast.155, bf16[4,10,256,384]{3,2,1,0:T(8,128)(2,1)S(1)} %copy-done.1, pred[4]{0:T(512)(128)(4,1)S(1)} %copy-done.13), kind=kOutput, calls=%fused_computation.113 | convolution fusion | flops 809238528 | bytes 12157440 | tf_op jit(solution)/shard_map/frwk,kc->frwc/dot_general | solution.py:76
  156.5 8.9 %gather_fusion = bf16[4,10,256,384]{3,2,1,0:T(8,128)(2,1)} fusion(bf16[6,10,256,384]{3,2,1,0:T(8,128)(2,1)} %pad_maximum_fusion, s32[1024]{0:T(1024)S(1)} %pad_clamp_fusion.2), kind=kCustom, calls=%fused_computation.clone | custom fusion | bytes 15728656 | tf_op jit(solution)/shard_map/jit(_take)/gather | solution.py:71
  165.4 6.8 %fusion.86 = f32[4,8,256,128]{3,2,1,0:T(8,128)} fusion(bf16[3,3,384,128]{3,2,1,0:T(8,128)(2,1)S(1)} %bitcast.156, bf16[4,10,256,384]{3,2,1,0:T(8,128)(2,1)} %gather_fusion, pred[4]{0:T(512)(128)(4,1)S(1)} %copy-done.11), kind=kOutput, calls=%fused_computation.115 | convolution fusion | flops 809238528 | bytes 12157440 | tf_op jit(solution)/shard_map/frwk,kc->frwc/dot_general | solution.py:76
  172.2 3.9 %fusion.87 = f32[4,8,256,128]{3,2,1,0:T(8,128)} fusion(bf16[3,3,384,128]{3,2,1,0:T(8,128)(2,1)S(1)} %bitcast.157, bf16[4,10,256,384]{3,2,1,0:T(8,128)(2,1)S(1)} %copy-done.2, pred[4]{0:T(512)(128)(4,1)S(1)} %copy-done.11), kind=kOutput, calls=%fused_computation.117 | convolution fusion | flops 809238528 | bytes 12157440 | tf_op jit(solution)/shard_map/frwk,kc->frwc/dot_general | solution.py:76
  176.0 3.9 %fusion.88 = f32[4,8,256,128]{3,2,1,0:T(8,128)} fusion(bf16[3,3,384,128]{3,2,1,0:T(8,128)(2,1)S(1)} %bitcast.158, bf16[4,10,256,384]{3,2,1,0:T(8,128)(2,1)S(1)} %copy-done.2, pred[4]{0:T(512)(128)(4,1)S(1)} %copy-done.11), kind=kOutput, calls=%fused_computation.119 | convolution fusion | flops 809238528 | bytes 12157440 | tf_op jit(solution)/shard_map/frwk,kc->frwc/dot_general | solution.py:76
  179.9 9.1 %gather_fusion.2 = bf16[4,10,256,384]{3,2,1,0:T(8,128)(2,1)} fusion(bf16[6,10,256,384]{3,2,1,0:T(8,128)(2,1)} %pad_maximum_fusion, s32[1024]{0:T(1024)S(1)} %pad_clamp_fusion), kind=kCustom, calls=%fused_computation.3.clone | custom fusion | bytes 15728656 | tf_op jit(solution)/shard_map/jit(_take)/gather | solution.py:71
  189.0 6.8 %fusion.82 = f32[4,8,256,128]{3,2,1,0:T(8,128)} fusion(bf16[3,3,384,128]{3,2,1,0:T(8,128)(2,1)S(1)} %bitcast.159, bf16[4,10,256,384]{3,2,1,0:T(8,128)(2,1)} %gather_fusion.2, pred[4]{0:T(512)(128)(4,1)S(1)} %get-tuple-element.23), kind=kOutput, calls=%fused_computation.107 | convolution fusion | flops 809238528 | bytes 12157440 | tf_op jit(solution)/shard_map/frwk,kc->frwc/dot_general | solution.py:76
  195.8 3.8 %fusion.81 = f32[4,8,256,128]{3,2,1,0:T(8,128)} fusion(bf16[3,3,384,128]{3,2,1,0:T(8,128)(2,1)S(1)} %bitcast.160, bf16[4,10,256,384]{3,2,1,0:T(8,128)(2,1)S(1)} %copy-done, pred[4]{0:T(512)(128)(4,1)S(1)} %get-tuple-element.23), kind=kOutput, calls=%fused_computation.105 | convolution fusion | flops 809238528 | bytes 12157440 | tf_op jit(solution)/shard_map/frwk,kc->frwc/dot_general | solution.py:76
  199.6 16.1 %fusion.21 = bf16[4,8,256,128]{3,2,1,0:T(8,128)(2,1)S(1)} fusion(bf16[4,8,256,128]{3,2,1,0:T(8,128)(2,1)} %param.12, f32[4,8,256,128]{3,2,1,0:T(8,128)} %fusion.81, f32[4,8,256,128]{3,2,1,0:T(8,128)} %fusion.82, f32[4,8,256,128]{3,2,1,0:T(8,128)} %fusion.83, f32[4,8,256,128]{3,2,1,0:T(8,128)} %fusion.84, f32[4,8,256,128]{3,2,1,0:T(8,128)} %fusion.85, ...), kind=kOutput, calls=%fused_computation.39 | convolution fusion | flops 821821440 | bytes 45712384 | tf_op jit(solution)/shard_map/frwk,kc->frwc/dot_general | solution.py:76
  217.8 14.2 %collective-permute-done.3 = bf16[2,8,256,128]{3,2,1,0:T(8,128)(2,1)S(1)} collective-permute-done((bf16[2,8,256,128]{3,2,1,0:T(8,128)(2,1)S(1)}, bf16[2,8,256,128]{3,2,1,0:T(8,128)(2,1)S(1)}, u32[]{:S(2)}, u32[]{:S(2)}) %collective-permute-start.3) | collective-permute-done | bytes 1048608 | tf_op jit(solution)/shard_map/ppermute | solution.py:32
  233.9 12.6 %collective-permute-done.4 = bf16[6,1,256,128]{3,2,1,0:T(8,128)(2,1)S(1)} collective-permute-done((bf16[6,1,256,128]{3,2,1,0:T(8,128)(2,1)S(1)}, bf16[6,1,256,128]{3,2,1,0:T(8,128)(2,1)S(1)}, u32[]{:S(2)}, u32[]{:S(2)}) %collective-permute-start.4) | collective-permute-done | bytes 393248 | tf_op jit(solution)/shard_map/ppermute | solution.py:32
  246.6 4.2 %fusion.31 = bf16[6,9,257,128]{3,2,1,0:T(8,128)(2,1)} fusion(bf16[6,1,256,128]{3,2,1,0:T(8,128)(2,1)S(1)} %maximum_select_fusion, bf16[4,8,256,128]{3,2,1,0:T(8,128)(2,1)S(1)} %fusion.21, bf16[2,8,256,128]{3,2,1,0:T(8,128)(2,1)S(1)} %collective-permute-done.3), kind=kLoop, calls=%fused_computation.55 | loop fusion | flops 28422144 | bytes 7091712 | tf_op jit(solution)/shard_map/jit(_pad)/concatenate | solution.py:136
  250.7 14.9 %slice.202 = bf16[6,9,128,128]{3,2,1,0:T(8,128)(2,1)S(1)} slice(bf16[6,9,257,128]{3,2,1,0:T(8,128)(2,1)} %fusion.31), slice={[0:6:1], [0:9:1], [0:255:2], [0:128:1]} | slice | bytes 3538944 | tf_op jit(solution)/shard_map/slice | solution.py:138
  265.6 14.9 %slice.203 = bf16[6,9,128,128]{3,2,1,0:T(8,128)(2,1)S(1)} slice(bf16[6,9,257,128]{3,2,1,0:T(8,128)(2,1)} %fusion.31), slice={[0:6:1], [0:9:1], [1:256:2], [0:128:1]} | slice | bytes 3538944 | tf_op jit(solution)/shard_map/slice | solution.py:138
  280.5 16.6 %slice.204 = bf16[6,9,128,128]{3,2,1,0:T(8,128)(2,1)} slice(bf16[6,9,257,128]{3,2,1,0:T(8,128)(2,1)} %fusion.31), slice={[0:6:1], [0:9:1], [2:257:2], [0:128:1]} | slice | bytes 3538944 | tf_op jit(solution)/shard_map/slice | solution.py:138
  297.1 4.3 %pad_maximum_fusion.1 = bf16[6,9,128,384]{3,2,1,0:T(8,128)(2,1)} fusion(bf16[6,9,128,128]{3,2,1,0:T(8,128)(2,1)} %slice.204, bf16[6,9,128,128]{3,2,1,0:T(8,128)(2,1)S(1)} %slice.203, bf16[6,9,128,128]{3,2,1,0:T(8,128)(2,1)S(1)} %slice.202), kind=kLoop, calls=%fused_computation.28 | loop fusion | flops 15925248 | bytes 10616832 | tf_op jit(solution)/shard_map/concatenate | solution.py:137
  301.5 3.8 %gather_fusion.4 = bf16[4,9,128,384]{3,2,1,0:T(8,128)(2,1)S(1)} fusion(bf16[6,9,128,384]{3,2,1,0:T(8,128)(2,1)} %pad_maximum_fusion.1, s32[1024]{0:T(1024)S(1)} %pad_clamp_fusion.1), kind=kCustom, calls=%fused_computation.4.clone | custom fusion | bytes 7077904 | tf_op jit(solution)/shard_map/jit(_take)/gather | solution.py:71
  306.4 2.5 fusion.39
  313.8 5.4 %gather_fusion.3 = bf16[4,9,128,384]{3,2,1,0:T(8,128)(2,1)} fusion(bf16[6,9,128,384]{3,2,1,0:T(8,128)(2,1)} %pad_maximum_fusion.1, s32[1024]{0:T(1024)S(1)} %pad_clamp_fusion.2), kind=kCustom, calls=%fused_computation.1.clone | custom fusion | bytes 7077904 | tf_op jit(solution)/shard_map/jit(_take)/gather | solution.py:71
  326.6 5.4 %gather_fusion.5 = bf16[4,9,128,384]{3,2,1,0:T(8,128)(2,1)} fusion(bf16[6,9,128,384]{3,2,1,0:T(8,128)(2,1)} %pad_maximum_fusion.1, s32[1024]{0:T(1024)S(1)} %pad_clamp_fusion), kind=kCustom, calls=%fused_computation.5.clone | custom fusion | bytes 7077904 | tf_op jit(solution)/shard_map/jit(_take)/gather | solution.py:71
  339.1 2.6 fusion.78
  (74 shorter events, 38.3 us)
Async XLA Ops:
  73.9 16.1 %collective-permute-start = (bf16[2,8,256,128]{3,2,1,0:T(8,128)(2,1)S(1)}, bf16[2,8,256,128]{3,2,1,0:T(8,128)(2,1)S(1)}, u32[]{:S(2)}, u32[]{:S(2)}) collective-permute-start(bf16[2,8,256,128]{3,2,1,0:T(8,128)(2,1)S(1)} %slice.235), channel_id=1, source_target_pairs={{0,16},{16,32},{32,48},{48,64},{64,80},{80,96},{96,112},{1,17},{17... | collective-permute-start | bytes 3145736 | tf_op jit(solution)/shard_map/ppermute | solution.py:32
  90.0 4.9 %copy-start.8 = (bf16[6,1,256,128]{3,2,1,0:T(8,128)(2,1)}, bf16[6,1,256,128]{3,2,1,0:T(8,128)(2,1)S(1)}, u32[]{:S(2)}) copy-start(bf16[6,1,256,128]{3,2,1,0:T(8,128)(2,1)S(1)} %pad_maximum_fusion.10) | copy-start | bytes 1179652
  90.0 12.1 %collective-permute-start.2 = (bf16[6,1,256,128]{3,2,1,0:T(8,128)(2,1)S(1)}, bf16[6,1,256,128]{3,2,1,0:T(8,128)(2,1)}, u32[]{:S(2)}, u32[]{:S(2)}) collective-permute-start(bf16[6,1,256,128]{3,2,1,0:T(8,128)(2,1)S(1)} %pad_maximum_fusion.10), channel_id=1, source_target_pairs={{1,0},{2,1},{3,2},{4,3},{5,4},{6,5},{7,6},{8,7},{9,8},{10,9},{11,1... | collective-permute-start | bytes 1179656 | tf_op jit(solution)/shard_map/ppermute | solution.py:22
  103.9 13.9 %collective-permute-start.1 = (bf16[6,1,256,128]{3,2,1,0:T(8,128)(2,1)}, bf16[6,1,256,128]{3,2,1,0:T(8,128)(2,1)}, u32[]{:S(2)}, u32[]{:S(2)}) collective-permute-start(bf16[6,1,256,128]{3,2,1,0:T(8,128)(2,1)} %get-tuple-element.20), channel_id=1, source_target_pairs={{0,1},{1,2},{2,3},{3,4},{4,5},{5,6},{6,7},{7,8},{8,9},{9,10},{10,1... | collective-permute-start | bytes 1179656 | tf_op jit(solution)/shard_map/ppermute | solution.py:20
  132.5 9.2 %copy-start.9 = (bf16[3,3,3,128,128]{4,3,2,1,0:T(8,128)(2,1)S(1)}, bf16[3,3,3,128,128]{4,3,2,1,0:T(8,128)(2,1)}, u32[]{:S(2)}) copy-start(bf16[3,3,3,128,128]{4,3,2,1,0:T(8,128)(2,1)} %param.16) | copy-start | bytes 2654212
  132.5 9.2 %copy-start.13 = (pred[4]{0:T(512)(128)(4,1)S(1)}, pred[4]{0:T(512)(128)(4,1)}, u32[]{:S(2)}) copy-start(pred[4]{0:T(512)(128)(4,1)} %get-tuple-element.25) | copy-start | bytes 16
  141.8 6.8 %copy-start.1 = (bf16[4,10,256,384]{3,2,1,0:T(8,128)(2,1)S(1)}, bf16[4,10,256,384]{3,2,1,0:T(8,128)(2,1)}, u32[]{:S(2)}) copy-start(bf16[4,10,256,384]{3,2,1,0:T(8,128)(2,1)} %gather_fusion.1) | copy-start | bytes 23592964
  156.5 8.9 %copy-start.11 = (pred[4]{0:T(512)(128)(4,1)S(1)}, pred[4]{0:T(512)(128)(4,1)}, u32[]{:S(2)}) copy-start(pred[4]{0:T(512)(128)(4,1)} %get-tuple-element.11) | copy-start | bytes 16
  165.4 6.8 %copy-start.2 = (bf16[4,10,256,384]{3,2,1,0:T(8,128)(2,1)S(1)}, bf16[4,10,256,384]{3,2,1,0:T(8,128)(2,1)}, u32[]{:S(2)}) copy-start(bf16[4,10,256,384]{3,2,1,0:T(8,128)(2,1)} %gather_fusion) | copy-start | bytes 23592964
  189.0 6.8 %copy-start = (bf16[4,10,256,384]{3,2,1,0:T(8,128)(2,1)S(1)}, bf16[4,10,256,384]{3,2,1,0:T(8,128)(2,1)}, u32[]{:S(2)}) copy-start(bf16[4,10,256,384]{3,2,1,0:T(8,128)(2,1)} %gather_fusion.2) | copy-start | bytes 23592964
  195.8 3.8 %copy-start.10 = (f32[128]{0:T(128)S(1)}, f32[128]{0:T(128)}, u32[]{:S(2)}) copy-start(f32[128]{0:T(128)} %param.17) | copy-start | bytes 1540
  215.8 16.1 %collective-permute-start.3 = (bf16[2,8,256,128]{3,2,1,0:T(8,128)(2,1)S(1)}, bf16[2,8,256,128]{3,2,1,0:T(8,128)(2,1)S(1)}, u32[]{:S(2)}, u32[]{:S(2)}) collective-permute-start(bf16[2,8,256,128]{3,2,1,0:T(8,128)(2,1)S(1)} %slice.245), channel_id=1, source_target_pairs={{0,16},{16,32},{32,48},{48,64},{64,80},{80,96},{96,112},{1,17},{17... | collective-permute-start | bytes 3145736 | tf_op jit(solution)/shard_map/ppermute | solution.py:32
  232.0 14.5 %collective-permute-start.4 = (bf16[6,1,256,128]{3,2,1,0:T(8,128)(2,1)S(1)}, bf16[6,1,256,128]{3,2,1,0:T(8,128)(2,1)S(1)}, u32[]{:S(2)}, u32[]{:S(2)}) collective-permute-start(bf16[6,1,256,128]{3,2,1,0:T(8,128)(2,1)S(1)} %pad_maximum_fusion.8), channel_id=1, source_target_pairs={{0,1},{1,2},{2,3},{3,4},{4,5},{5,6},{6,7},{7,8},{8,9},{9,10},{10,1... | collective-permute-start | bytes 1179656 | tf_op jit(solution)/shard_map/ppermute | solution.py:32
  313.8 5.4 %copy-start.12 = (pred[4]{0:T(512)(128)(4,1)S(1)}, pred[4]{0:T(512)(128)(4,1)}, u32[]{:S(2)}) copy-start(pred[4]{0:T(512)(128)(4,1)} %get-tuple-element.11) | copy-start | bytes 16
  334.4 4.6 %copy-start.3 = (f32[4,4,128,128]{3,2,1,0:T(8,128)S(1)}, f32[4,4,128,128]{3,2,1,0:T(8,128)}, u32[]{:S(2)}) copy-start(f32[4,4,128,128]{3,2,1,0:T(8,128)} %fusion.39) | copy-start | bytes 3145732
  334.4 4.6 %copy-start.4 = (f32[4,4,128,128]{3,2,1,0:T(8,128)S(1)}, f32[4,4,128,128]{3,2,1,0:T(8,128)}, u32[]{:S(2)}) copy-start(f32[4,4,128,128]{3,2,1,0:T(8,128)} %fusion.41) | copy-start | bytes 3145732
  334.5 4.6 %copy-start.5 = (f32[4,4,128,128]{3,2,1,0:T(8,128)S(1)}, f32[4,4,128,128]{3,2,1,0:T(8,128)}, u32[]{:S(2)}) copy-start(f32[4,4,128,128]{3,2,1,0:T(8,128)} %fusion.43) | copy-start | bytes 3145732
  334.5 4.6 %copy-start.6 = (f32[4,4,128,128]{3,2,1,0:T(8,128)S(1)}, f32[4,4,128,128]{3,2,1,0:T(8,128)}, u32[]{:S(2)}) copy-start(f32[4,4,128,128]{3,2,1,0:T(8,128)} %fusion.45) | copy-start | bytes 3145732
  334.5 4.6 %copy-start.7 = (f32[4,4,128,128]{3,2,1,0:T(8,128)S(1)}, f32[4,4,128,128]{3,2,1,0:T(8,128)}, u32[]{:S(2)}) copy-start(f32[4,4,128,128]{3,2,1,0:T(8,128)} %fusion.47) | copy-start | bytes 3145732
  334.5 4.6 %copy-start.14 = (f32[128]{0:T(128)S(1)}, f32[128]{0:T(128)}, u32[]{:S(2)}) copy-start(f32[128]{0:T(128)} %param.19) | copy-start | bytes 1540
where the time goes:
time: 344 us; the launch traced here: 342 us
  local copies, waits for them, and re-layouts  89.1 us (26%)
  matrix products  76.1 us (22%)
  blocking collectives  65.2 us (19%)
  waiting for transfers between devices  58.4 us (17%)
  other arithmetic  39.5 us (11%)
  starting transfers between devices  13 us (4%)
    dot_general x18, matrix products, conv_taps(): jnp.einsum('frwk,kc->frwc', sliced, kernel[time_tap, row_tap], preferred_...  75.3 us
    psum x1, blocking collectives, per_device(): clip_sum, clip_square = lax.psum((clip_sum, clip_square), ('tm', 'rows'))  65.2 us
    slice x3, local copies, waits for them, and re-layouts, per_device(): padded[:, :, col_tap:col_tap + columns - 1:2]  46.4 us
    gather x6, local copies, waits for them, and re-layouts, conv_taps(): picked = jnp.take(widened, sources[:, time_tap], axis=0)  41.9 us
    ppermute x3, waiting for transfers between devices, passed_along(): lax.ppermute(value, axis, [(source, source + steps) for source in range(f...  41 us
    ppermute x1, waiting for transfers between devices, with_halo(): lax.ppermute(tail, axis, [(i, (i + 1) % count) for i in range(ends)])  10.3 us
    ppermute x1, waiting for transfers between devices, with_halo(): lax.ppermute(head, axis, [((i + 1) % count, i) for i in range(ends)])  7.12 us
    concatenate x1, other arithmetic, widen_columns(): padded = jnp.pad(frame_block, ((0, 0), (0, 0), (1, 1), (0, 0)), mode='edge')  7.08 us
  transfers between devices with their start and end apart: 5, of which 5 were waited for; matrix products, arithmetic and copies ran while one was open for 0% of the time, Pallas kernels for 0%

commit v1 on v0

v1 whole, which is shorter than its diff:
```python
import jax
import jax.numpy as jnp
from jax import lax
from jax.experimental import pallas as pl
from jax.experimental.pallas import tpu as pltpu
from jax.sharding import PartitionSpec as P

GROUPS = 32
EPSILON = 1e-06
TM, ROWS = 8, 16
FRAMES, BAND, COLS, CH = 4, 8, 256, 128
HEIGHT = BAND * ROWS
PER_GROUP = CH // GROUPS
EXT = FRAMES + 2
OUT_ROWS, OUT_COLS = BAND // 2, COLS // 2
F32, BF16 = jnp.float32, jnp.bfloat16


def kernel(
    video, clip, gain, shift, cw_hbm, cbias, dw_hbm, dbias, out,
    raw, hid, cw, dw, wc, wd, part, tot, rbuf, tbuf, mom, coef, hs, ss, dn,
    rowsend, rowrecv, z, psend, precv,
    load_sem, halo_send, halo_recv, r_send, r_recv, t_send, t_recv,
    row_send, row_recv, p_send, p_recv,
):
    d = lax.axis_index("tm")
    r = lax.axis_index("rows")

    def tm(k):
        return lax.rem(d + (k + TM), TM)

    def rw(k):
        return lax.rem(r + (k + ROWS), ROWS)

    def remote(src, dst, send, recv, k, j):
        return pltpu.make_async_remote_copy(
            src_ref=src, dst_ref=dst, send_sem=send, recv_sem=recv,
            device_id=(tm(k), rw(j)), device_id_type=pl.DeviceIdType.MESH,
        )

    loads = [
        pltpu.make_async_copy(video.at[f], raw.at[2 + f, pl.ds(1, BAND)], load_sem.at[f])
        for f in range(FRAMES)
    ]
    loads.append(pltpu.make_async_copy(cw_hbm, cw, load_sem.at[FRAMES]))
    loads.append(pltpu.make_async_copy(dw_hbm, dw, load_sem.at[FRAMES + 1]))
    for copy in loads:
        copy.start()

    barrier = pltpu.get_barrier_semaphore()
    peers = [(0, j) for j in range(1, ROWS)] + [(k, 0) for k in (-2, -1, 1, 2)]
    peers += [(1, 1), (1, -1), (-1, 1), (-1, -1)]
    for k, j in peers:
        pl.semaphore_signal(
            barrier, inc=1, device_id=(tm(k), rw(j)), device_id_type=pl.DeviceIdType.MESH
        )
    pl.semaphore_wait(barrier, len(peers))

    halos = [
        remote(video.at[pl.ds(2, 2)], raw.at[pl.ds(0, 2), pl.ds(1, BAND)], halo_send.at[0], halo_recv.at[0], 1, 0),
        remote(video.at[:, BAND - 1], raw.at[pl.ds(2, FRAMES), 0], halo_send.at[1], halo_recv.at[1], 0, 1),
        remote(video.at[:, 0], raw.at[pl.ds(2, FRAMES), BAND + 1], halo_send.at[2], halo_recv.at[2], 0, -1),
        remote(video.at[pl.ds(2, 2), BAND - 1], raw.at[pl.ds(0, 2), 0], halo_send.at[3], halo_recv.at[3], 1, 1),
        remote(video.at[pl.ds(2, 2), 0], raw.at[pl.ds(0, 2), BAND + 1], halo_send.at[4], halo_recv.at[4], 1, -1),
    ]
    for copy in halos:
        copy.start()

    for f in range(FRAMES):
        loads[f].wait()

        def add_row(i, sums, f=f):
            x = raw[2 + f, 1 + i].astype(F32).reshape(COLS // 8, 8, CH)
            return sums[0] + jnp.sum(x, axis=0), sums[1] + jnp.sum(x * x, axis=0)

        zero = jnp.zeros((8, CH), F32)
        s, q = lax.fori_loop(0, BAND, add_row, (zero, zero))
        part[pl.ds(f, 1)] = jnp.sum(s, axis=0, keepdims=True)
        part[pl.ds(FRAMES + f, 1)] = jnp.sum(q, axis=0, keepdims=True)

    rcopies = [
        remote(part, rbuf.at[j], r_send.at[j], r_recv.at[j], 0, j) for j in range(1, ROWS)
    ]
    for copy in rcopies:
        copy.start()

    loads[FRAMES].wait()
    loads[FRAMES + 1].wait()

    def lay_conv(a, carry):
        for rr in range(4):
            for e in range(3):
                at = pl.ds((rr * 3 + e) * CH, CH)
                empty = jnp.zeros((CH, CH), BF16)
                wc[a, at, pl.ds(0, CH)] = cw[a, rr, e] if rr < 3 else empty
                wc[a, at, pl.ds(CH, CH)] = cw[a, rr - 1, e] if rr > 0 else empty
        return carry

    lax.fori_loop(0, 3, lay_conv, 0)
    for a in range(3):
        for be in range(9):
            wd[pl.ds(be * CH, CH), pl.ds(a * CH, CH)] = dw[a, be // 3, be % 3]

    base = d * FRAMES - 2
    firsts, ends = [], []
    for e in range(EXT + 1):
        first, end, start = jnp.int32(0), jnp.int32(0), jnp.int32(0)
        for c in range(8):
            stop = start + clip[c]
            inside = (base + e >= start) & (base + e < stop)
            first = jnp.where(inside, start, first)
            end = jnp.where(inside, stop, end)
            start = stop
        firsts.append(first - base)
        ends.append(end - base)

    rbuf[0] = part[...]
    for copy in rcopies:
        copy.wait_recv()
    total = rbuf[0]
    for j in range(1, ROWS):
        total = total + rbuf[j]
    tot[...] = total
    tbuf[2] = total
    tcopies = [
        remote(tot, tbuf.at[2 - k], t_send.at[2 - k], t_recv.at[2 - k], k, 0)
        for k in (-2, -1, 1, 2)
    ]
    for copy in tcopies:
        copy.start()
    for copy in tcopies:
        copy.wait_recv()

    sub = lax.broadcasted_iota(jnp.int32, (8, CH), 0)
    mom[...] = jnp.zeros((16, CH), F32)
    count = jnp.ones((8, CH), F32)
    for e in range(EXT):
        mine = jnp.zeros((8, CH), F32)
        for k in range(5):
            at = lax.rem(sub, FRAMES) + (2 + (k - 2) * FRAMES)
            mine = mine + jnp.where((at >= firsts[e]) & (at < ends[e]), tbuf[k], 0.0)
        mom[pl.ds(e, 1)] = jnp.sum(jnp.where(sub < FRAMES, mine, 0.0), axis=0, keepdims=True)
        mom[pl.ds(8 + e, 1)] = jnp.sum(jnp.where(sub >= FRAMES, mine, 0.0), axis=0, keepdims=True)
        frames = jnp.maximum(ends[e] - firsts[e], 1)
        count = jnp.where(sub == e, (frames * (HEIGHT * COLS * PER_GROUP)).astype(F32), count)
    lane_a = lax.broadcasted_iota(jnp.int32, (CH, CH), 0) // PER_GROUP
    lane_b = lax.broadcasted_iota(jnp.int32, (CH, CH), 1) // PER_GROUP
    same = jnp.where(lane_a == lane_b, 1.0, 0.0).astype(F32)
    grouped = jnp.dot(
        mom[...], same, preferred_element_type=F32, precision=lax.Precision.HIGHEST
    )
    mean = grouped[0:8] / count
    scale = lax.rsqrt(grouped[8:16] / count - mean * mean + EPSILON)
    slope = scale * gain[...]
    coef[0] = 0.5 * slope
    coef[1] = 0.5 * (shift[...] - mean * slope)

    def activate(f, n):
        def row(i, carry):
            pick = jnp.where((i == 0) & (r == 0), 1, i)
            pick = jnp.where((i == BAND + 1) & (r == ROWS - 1), BAND, pick)
            x = raw[f, pick].astype(F32)
            h = x * coef[0, pl.ds(f, 1)] + coef[1, pl.ds(f, 1)]
            v = h * jnp.tanh(h) + h
            hs[pl.ds(8, COLS)] = v
            hs[pl.ds(7, 1)] = v[0:1]
            hs[pl.ds(8 + COLS, 1)] = v[COLS - 1:COLS]
            hid[f, i, :, pl.ds(0, CH)] = hs[pl.ds(7, COLS)].astype(BF16)
            hid[f, i, :, pl.ds(CH, CH)] = v.astype(BF16)
            hid[f, i, :, pl.ds(2 * CH, CH)] = hs[pl.ds(9, COLS)].astype(BF16)
            return carry

        lax.fori_loop(0, BAND + 2, row, 0)

    def spread(y, f, row, slot):
        ss[slot, pl.ds(8, COLS)] = y
        ss[slot, pl.ds(7, 1)] = y[0:1]
        for e in range(3):
            dn[f, row, :, pl.ds(e * CH, CH)] = ss[slot, pl.ds(7 + e, OUT_COLS, stride=2)].astype(BF16)

    rowcopies = [
        remote(rowsend.at[pl.ds(2, 2)], rowrecv.at[pl.ds(2, 2)], row_send.at[0], row_recv.at[0], 0, 1),
        remote(rowsend.at[pl.ds(0, 2)], rowrecv.at[pl.ds(0, 2)], row_send.at[1], row_recv.at[1], 0, 1),
    ]

    def convolve(pair):
        def step(n, carry):
            p = BAND // 2 - 1 - n
            for f in pair:
                acc = None
                for a in range(3):
                    at = jnp.maximum(f - 2 + a, firsts[f])
                    taps = jnp.concatenate([hid[at, 2 * p + rr] for rr in range(4)], axis=-1)
                    term = jnp.dot(taps, wc[a], preferred_element_type=F32)
                    acc = term if acc is None else acc + term
                for half in range(2):
                    y = acc[:, half * CH:(half + 1) * CH] + cbias[...]
                    y = y + raw[f, 2 * p + 1 + half].astype(F32)
                    spread(y, f - 2, 2 * p + 1 + half, half)
                    if half == 1:
                        @pl.when(n == 0)
                        def _(y=y, f=f):
                            rowsend[f - 2] = y.astype(BF16)

            @pl.when(n == 0)
            def _():
                rowcopies[0 if pair[0] == 4 else 1].start()

            return carry

        lax.fori_loop(0, BAND // 2, step, 0)

    def upper(pair):
        rowcopies[0 if pair[0] == 4 else 1].wait_recv()
        for f in pair:
            spread(rowrecv[f - 2].astype(F32), f - 2, 0, 0)

            @pl.when(r == 0)
            def _(f=f):
                dn[f - 2, 0] = dn[f - 2, 1]

    def downsample(s):
        taps = jnp.concatenate(
            [
                jnp.concatenate([dn[s, 2 * i + b] for b in range(3)], axis=-1)
                for i in range(OUT_ROWS)
            ],
            axis=0,
        )
        z[s] = jnp.dot(taps, wd[...], preferred_element_type=F32)

    lane = [pl.ds(a * CH, CH) for a in range(3)]

    halos[1].wait_recv()
    halos[2].wait_recv()
    for f in range(2, EXT):
        activate(f, BAND + 2)
    convolve((4, 5))
    upper((4, 5))
    downsample(2)
    downsample(3)
    ahead = jnp.minimum(jnp.maximum(firsts[EXT] - 2, 2), 3)
    psend[0] = z[3, :, lane[1]] + z[ahead, :, lane[0]]
    psend[1] = z[3, :, lane[0]]
    pcopy = remote(psend, precv, p_send.at[0], p_recv.at[0], 1, 0)
    pcopy.start()

    for j in (0, 3, 4):
        halos[j].wait_recv()
    for f in range(2):
        activate(f, BAND + 2)
    convolve((2, 3))
    upper((2, 3))
    downsample(0)
    downsample(1)
    pcopy.wait_recv()

    for t in range(FRAMES):
        first = firsts[t + 2] - 2
        total = z[t, :, lane[2]] + dbias[...]
        one = jnp.maximum(jnp.maximum(t - 1, first), 0)
        two = jnp.maximum(jnp.maximum(t - 2, first), 0)
        if t == 0:
            rest = jnp.where(first < 0, precv[0], z[0, :, lane[1]] + z[0, :, lane[0]])
        elif t == 1:
            rest = z[one, :, lane[1]] + jnp.where(first < 0, precv[1], z[two, :, lane[0]])
        else:
            rest = z[one, :, lane[1]] + z[two, :, lane[0]]
        out[t] = (total + rest).astype(BF16).reshape(OUT_ROWS, OUT_COLS, CH)

    for copy in halos + rcopies + tcopies + rowcopies + [pcopy]:
        copy.wait_send()


def per_device(video, clip_lengths, gain, shift, conv_weight, conv_bias, down_weight, down_bias):
    any_space = pl.BlockSpec(memory_space=pl.ANY)
    vmem = pl.BlockSpec(memory_space=pltpu.VMEM)
    smem = pl.BlockSpec(memory_space=pltpu.SMEM)
    dma = pltpu.SemaphoreType.DMA
    pixels = OUT_ROWS * OUT_COLS
    return pl.pallas_call(
        kernel,
        out_shape=jax.ShapeDtypeStruct((FRAMES, OUT_ROWS, OUT_COLS, CH), BF16),
        in_specs=[any_space, smem, vmem, vmem, any_space, vmem, any_space, vmem],
        out_specs=vmem,
        scratch_shapes=[
            pltpu.VMEM((EXT, BAND + 2, COLS, CH), BF16),
            pltpu.VMEM((EXT, BAND + 2, COLS, 3 * CH), BF16),
            pltpu.VMEM((3, 3, 3, CH, CH), BF16),
            pltpu.VMEM((3, 3, 3, CH, CH), BF16),
            pltpu.VMEM((3, 12 * CH, 2 * CH), BF16),
            pltpu.VMEM((9 * CH, 3 * CH), BF16),
            pltpu.VMEM((8, CH), F32),
            pltpu.VMEM((8, CH), F32),
            pltpu.VMEM((ROWS, 8, CH), F32),
            pltpu.VMEM((5, 8, CH), F32),
            pltpu.VMEM((16, CH), F32),
            pltpu.VMEM((2, 8, CH), F32),
            pltpu.VMEM((COLS + 16, CH), F32),
            pltpu.VMEM((2, COLS + 8, CH), F32),
            pltpu.VMEM((FRAMES, BAND + 1, OUT_COLS, 3 * CH), BF16),
            pltpu.VMEM((FRAMES, COLS, CH), BF16),
            pltpu.VMEM((FRAMES, COLS, CH), BF16),
            pltpu.VMEM((FRAMES, pixels, 3 * CH), F32),
            pltpu.VMEM((2, pixels, CH), F32),
            pltpu.VMEM((2, pixels, CH), F32),
            dma((FRAMES + 2,)),
            dma((5,)), dma((5,)),
            dma((ROWS,)), dma((ROWS,)),
            dma((5,)), dma((5,)),
            dma((2,)), dma((2,)),
            dma((1,)), dma((1,)),
        ],
        compiler_params=pltpu.CompilerParams(
            collective_id=0, has_side_effects=True, vmem_limit_bytes=56 * 1024 * 1024
        ),
        cost_estimate=pl.CostEstimate(
            flops=9_060_000_000, bytes_accessed=5_000_000, transcendentals=2_000_000
        ),
        name="encode",
    )(
        video, clip_lengths, gain.reshape(1, CH), shift.reshape(1, CH),
        conv_weight, conv_bias.reshape(1, CH), down_weight, down_bias.reshape(1, CH),
    )


def solution(mesh):
    placed = (P("tm", "rows", None, None), P(), P(), P(), P(), P(), P(), P())
    return jax.shard_map(
        per_device, mesh=mesh, in_specs=placed,
        out_specs=P("tm", "rows", None, None), check_vma=False,
    )
```

time: 344 us -> 59.8 us (0.17)
  the two profiles are of different devices: /device:TPU:40 before, /device:TPU:0 now
where the time goes in v1:
time: 59.8 us; the launch traced here: 58.6 us
  Pallas kernels  56.7 us (95%)
  local copies, waits for them, and re-layouts  1.89 us (3%)
    pallas_call x1, Pallas kernels, per_device(): pl.pallas_call(kernel, out_shape=jax.ShapeDtypeStruct((FRAMES, OUT_ROWS,...  56.7 us
    unnamed x1, local copies, waits for them, and re-layouts  1.89 us

profile of v1, /device:TPU:0, one launch (start us, length us, event | category | flops | bytes accessed | tf_op | source)
XLA Modules:
  0.0 58.6 jit_solution(1457614087587019555)
XLA Ops:
  0.0 56.7 %encode.1 = bf16[4,4,128,128]{3,2,1,0:T(8,128)(2,1)} custom-call(bf16[4,8,256,128]{3,2,1,0:T(8,128)(2,1)} %video.1, s32[8]{0:T(128)} %clip.1, f32[1,128]{1,0:T(1,128)} %bitcast.4, f32[1,128]{1,0:T(1,128)} %bitcast.5, bf16[3,3,3,128,128]{4,3,2,1,0:T(8,128)(2,1)} %cw_hbm.1, f32[1,128]{1,0:T(1,128)} %bitcast.6, bf16[3,3,3,128,128]{4,3,2,1,0:T(8,128)(2,1)} %dw_hbm.1, ...), custom_call_target="tpu_custom_call" | custom-call | flops 9059999744 | bytes 5000000 | tf_op jit(solution)/shard_map/encode/pallas_call | solution.py:281
  56.7 1.9 %copy.10 = bf16[4,4,128,128]{3,2,1,0:T(8,128)(2,1)} copy(bf16[4,4,128,128]{3,2,1,0:T(8,128)(2,1)} %encode.1) | data formatting | bytes 1048576

commit v2 on v1

--- a/solution.py
+++ b/solution.py
@@ -18,11 +18,12 @@
 
 def kernel(
     video, clip, gain, shift, cw_hbm, cbias, dw_hbm, dbias, out,
-    raw, hid, cw, dw, wc, wd, part, tot, rbuf, tbuf, mom, coef, hs, ss, dn,
+    raw, hid0, hid1, hid2, hid3, hid4, cw, dw, wc, wd, part, tot, rbuf, tbuf, mom, coef, hs, ss, dn,
     rowsend, rowrecv, z, psend, precv,
     load_sem, halo_send, halo_recv, r_send, r_recv, t_send, t_recv,
     row_send, row_recv, p_send, p_recv,
 ):
+    hid = (hid0, hid1, hid2, hid3, hid4)
     d = lax.axis_index("tm")
     r = lax.axis_index("rows")
 
@@ -54,17 +55,6 @@
         pl.semaphore_signal(
             barrier, inc=1, device_id=(tm(k), rw(j)), device_id_type=pl.DeviceIdType.MESH
         )
-    pl.semaphore_wait(barrier, len(peers))
-
-    halos = [
-        remote(video.at[pl.ds(2, 2)], raw.at[pl.ds(0, 2), pl.ds(1, BAND)], halo_send.at[0], halo_recv.at[0], 1, 0),
-        remote(video.at[:, BAND - 1], raw.at[pl.ds(2, FRAMES), 0], halo_send.at[1], halo_recv.at[1], 0, 1),
-        remote(video.at[:, 0], raw.at[pl.ds(2, FRAMES), BAND + 1], halo_send.at[2], halo_recv.at[2], 0, -1),
-        remote(video.at[pl.ds(2, 2), BAND - 1], raw.at[pl.ds(0, 2), 0], halo_send.at[3], halo_recv.at[3], 1, 1),
-        remote(video.at[pl.ds(2, 2), 0], raw.at[pl.ds(0, 2), BAND + 1], halo_send.at[4], halo_recv.at[4], 1, -1),
-    ]
-    for copy in halos:
-        copy.start()
 
     for f in range(FRAMES):
         loads[f].wait()
@@ -77,12 +67,6 @@
         s, q = lax.fori_loop(0, BAND, add_row, (zero, zero))
         part[pl.ds(f, 1)] = jnp.sum(s, axis=0, keepdims=True)
         part[pl.ds(FRAMES + f, 1)] = jnp.sum(q, axis=0, keepdims=True)
-
-    rcopies = [
-        remote(part, rbuf.at[j], r_send.at[j], r_recv.at[j], 0, j) for j in range(1, ROWS)
-    ]
-    for copy in rcopies:
-        copy.start()
 
     loads[FRAMES].wait()
     loads[FRAMES + 1].wait()
@@ -113,6 +97,24 @@
             start = stop
         firsts.append(first - base)
         ends.append(end - base)
+
+    pl.semaphore_wait(barrier, len(peers))
+
+    rcopies = [
+        remote(part, rbuf.at[j], r_send.at[j], r_recv.at[j], 0, j) for j in range(1, ROWS)
+    ]
+    for copy in rcopies:
+        copy.start()
+
+    halos = [
+        remote(video.at[pl.ds(2, 2)], raw.at[pl.ds(0, 2), pl.ds(1, BAND)], halo_send.at[0], halo_recv.at[0], 1, 0),
+        remote(video.at[:, BAND - 1], raw.at[pl.ds(2, FRAMES), 0], halo_send.at[1], halo_recv.at[1], 0, 1),
+        remote(video.at[:, 0], raw.at[pl.ds(2, FRAMES), BAND + 1], halo_send.at[2], halo_recv.at[2], 0, -1),
+        remote(video.at[pl.ds(2, 2), BAND - 1], raw.at[pl.ds(0, 2), 0], halo_send.at[3], halo_recv.at[3], 1, 1),
+        remote(video.at[pl.ds(2, 2), 0], raw.at[pl.ds(0, 2), BAND + 1], halo_send.at[4], halo_recv.at[4], 1, -1),
+    ]
+    for copy in halos:
+        copy.start()
 
     rbuf[0] = part[...]
     for copy in rcopies:
@@ -155,22 +157,25 @@
     coef[0] = 0.5 * slope
     coef[1] = 0.5 * (shift[...] - mean * slope)
 
-    def activate(f, n):
-        def row(i, carry):
-            pick = jnp.where((i == 0) & (r == 0), 1, i)
-            pick = jnp.where((i == BAND + 1) & (r == ROWS - 1), BAND, pick)
-            x = raw[f, pick].astype(F32)
-            h = x * coef[0, pl.ds(f, 1)] + coef[1, pl.ds(f, 1)]
-            v = h * jnp.tanh(h) + h
-            hs[pl.ds(8, COLS)] = v
-            hs[pl.ds(7, 1)] = v[0:1]
-            hs[pl.ds(8 + COLS, 1)] = v[COLS - 1:COLS]
-            hid[f, i, :, pl.ds(0, CH)] = hs[pl.ds(7, COLS)].astype(BF16)
-            hid[f, i, :, pl.ds(CH, CH)] = v.astype(BF16)
-            hid[f, i, :, pl.ds(2 * CH, CH)] = hs[pl.ds(9, COLS)].astype(BF16)
-            return carry
-
-        lax.fori_loop(0, BAND + 2, row, 0)
+    def activate(frames, group):
+        for f in frames:
+            for q in range(2):
+                i = 2 * group + q
+                pick = i
+                if i == 0:
+                    pick = jnp.where(r == 0, 1, 0)
+                if i == BAND + 1:
+                    pick = jnp.where(r == ROWS - 1, BAND, BAND + 1)
+                x = raw[f, pick].astype(F32)
+                h = x * coef[0, pl.ds(f, 1)] + coef[1, pl.ds(f, 1)]
+                v = h * jnp.tanh(h) + h
+                slot = 2 * (f % 2) + q
+                hs[slot, pl.ds(8, COLS)] = v
+                hs[slot, pl.ds(7, 1)] = v[0:1]
+                hs[slot, pl.ds(8 + COLS, 1)] = v[COLS - 1:COLS]
+                hid[group][f, q, :, pl.ds(0, CH)] = hs[slot, pl.ds(7, COLS)].astype(BF16)
+                hid[group][f, q, :, pl.ds(CH, CH)] = v.astype(BF16)
+                hid[group][f, q, :, pl.ds(2 * CH, CH)] = hs[slot, pl.ds(9, COLS)].astype(BF16)
 
     def spread(y, f, row, slot):
         ss[slot, pl.ds(8, COLS)] = y
@@ -183,35 +188,23 @@
         remote(rowsend.at[pl.ds(0, 2)], rowrecv.at[pl.ds(0, 2)], row_send.at[1], row_recv.at[1], 0, 1),
     ]
 
-    def convolve(pair):
-        def step(n, carry):
-            p = BAND // 2 - 1 - n
-            for f in pair:
-                acc = None
-                for a in range(3):
-                    at = jnp.maximum(f - 2 + a, firsts[f])
-                    taps = jnp.concatenate([hid[at, 2 * p + rr] for rr in range(4)], axis=-1)
-                    term = jnp.dot(taps, wc[a], preferred_element_type=F32)
-                    acc = term if acc is None else acc + term
-                for half in range(2):
-                    y = acc[:, half * CH:(half + 1) * CH] + cbias[...]
-                    y = y + raw[f, 2 * p + 1 + half].astype(F32)
-                    spread(y, f - 2, 2 * p + 1 + half, half)
-                    if half == 1:
-                        @pl.when(n == 0)
-                        def _(y=y, f=f):
-                            rowsend[f - 2] = y.astype(BF16)
-
-            @pl.when(n == 0)
-            def _():
-                rowcopies[0 if pair[0] == 4 else 1].start()
-
-            return carry
-
-        lax.fori_loop(0, BAND // 2, step, 0)
+    def convolve(f, p):
+        acc = None
+        for a in range(3):
+            at = jnp.maximum(f - 2 + a, firsts[f])
+            taps = jnp.concatenate(
+                [hid[p][at, 0], hid[p][at, 1], hid[p + 1][at, 0], hid[p + 1][at, 1]], axis=-1
+            )
+            term = jnp.dot(taps, wc[a], preferred_element_type=F32)
+            acc = term if acc is None else acc + term
+        for half in range(2):
+            y = acc[:, half * CH:(half + 1) * CH] + cbias[...]
+            y = y + raw[f, 2 * p + 1 + half].astype(F32)
+            spread(y, f - 2, 2 * p + 1 + half, half)
+            if p == BAND // 2 - 1 and half == 1:
+                rowsend[f - 2] = y.astype(BF16)
 
     def upper(pair):
-        rowcopies[0 if pair[0] == 4 else 1].wait_recv()
         for f in pair:
             spread(rowrecv[f - 2].astype(F32), f - 2, 0, 0)
 
@@ -219,41 +212,82 @@
             def _(f=f):
                 dn[f - 2, 0] = dn[f - 2, 1]
 
-    def downsample(s):
+    def downsample(frames, rows):
         taps = jnp.concatenate(
             [
                 jnp.concatenate([dn[s, 2 * i + b] for b in range(3)], axis=-1)
-                for i in range(OUT_ROWS)
+                for s in frames
+                for i in rows
             ],
             axis=0,
         )
-        z[s] = jnp.dot(taps, wd[...], preferred_element_type=F32)
+        res = jnp.dot(taps, wd[...], preferred_element_type=F32)
+        n = len(rows) * OUT_COLS
+        for k, s in enumerate(frames):
+            z[s, pl.ds(rows[0] * OUT_COLS, n)] = res[k * n:(k + 1) * n]
+
+    def partial_sums(start, n):
+        at = pl.ds(start, n)
+        psend[0, at] = z[3, at, lane[1]] + z[ahead, at, lane[0]]
+        psend[1, at] = z[3, at, lane[0]]
 
     lane = [pl.ds(a * CH, CH) for a in range(3)]
 
+    ahead = jnp.minimum(jnp.maximum(firsts[EXT] - 2, 2), 3)
+    own, late, early, before = (2, 3, 4, 5), (4, 5), (2, 3), (0, 1)
+    top, rest = pl.ds(0, OUT_COLS), pl.ds(OUT_COLS, 3 * OUT_COLS)
+    pcopies = [
+        remote(psend.at[:, rest], precv.at[:, rest], p_send.at[0], p_recv.at[0], 1, 0),
+        remote(psend.at[:, top], precv.at[:, top], p_send.at[1], p_recv.at[1], 1, 0),
+    ]
+
+    halos[2].wait_recv()
+    activate(own, 4)
+    activate(own, 3)
+    for f in late:
+        convolve(f, 3)
+    activate(own, 2)
+    rowcopies[0].start()
+    for f in late:
+        convolve(f, 2)
+    activate(own, 1)
     halos[1].wait_recv()
-    halos[2].wait_recv()
-    for f in range(2, EXT):
-        activate(f, BAND + 2)
-    convolve((4, 5))
-    upper((4, 5))
-    downsample(2)
-    downsample(3)
-    ahead = jnp.minimum(jnp.maximum(firsts[EXT] - 2, 2), 3)
-    psend[0] = z[3, :, lane[1]] + z[ahead, :, lane[0]]
-    psend[1] = z[3, :, lane[0]]
-    pcopy = remote(psend, precv, p_send.at[0], p_recv.at[0], 1, 0)
-    pcopy.start()
+    for f in late:
+        convolve(f, 1)
+    activate(own, 0)
+    for f in late:
+        convolve(f, 0)
+    downsample((2, 3), (1, 2, 3))
+    partial_sums(OUT_COLS, 3 * OUT_COLS)
+    pcopies[0].start()
 
     for j in (0, 3, 4):
         halos[j].wait_recv()
-    for f in range(2):
-        activate(f, BAND + 2)
-    convolve((2, 3))
-    upper((2, 3))
-    downsample(0)
-    downsample(1)
-    pcopy.wait_recv()
+    activate(before, 4)
+    activate(before, 3)
+    for f in early:
+        convolve(f, 3)
+    activate(before, 2)
+    rowcopies[1].start()
+    rowcopies[0].wait_recv()
+    upper(late)
+    downsample((2, 3), (0,))
+    partial_sums(0, OUT_COLS)
+    pcopies[1].start()
+    for f in early:
+        convolve(f, 2)
+    activate(before, 1)
+    for f in early:
+        convolve(f, 1)
+    activate(before, 0)
+    for f in early:
+        convolve(f, 0)
+    downsample((0, 1), (1, 2, 3))
+    rowcopies[1].wait_recv()
+    upper(early)
+    downsample((0, 1), (0,))
+    for copy in pcopies:
+        copy.wait_recv()
 
     for t in range(FRAMES):
         first = firsts[t + 2] - 2
@@ -268,7 +302,7 @@
             rest = z[one, :, lane[1]] + z[two, :, lane[0]]
         out[t] = (total + rest).astype(BF16).reshape(OUT_ROWS, OUT_COLS, CH)
 
-    for copy in halos + rcopies + tcopies + rowcopies + [pcopy]:
+    for copy in halos + rcopies + tcopies + rowcopies + pcopies:
         copy.wait_send()
 
 
@@ -285,7 +319,7 @@
         out_specs=vmem,
         scratch_shapes=[
             pltpu.VMEM((EXT, BAND + 2, COLS, CH), BF16),
-            pltpu.VMEM((EXT, BAND + 2, COLS, 3 * CH), BF16),
+            *[pltpu.VMEM((EXT, 2, COLS, 3 * CH), BF16)] * 5,
             pltpu.VMEM((3, 3, 3, CH, CH), BF16),
             pltpu.VMEM((3, 3, 3, CH, CH), BF16),
             pltpu.VMEM((3, 12 * CH, 2 * CH), BF16),
@@ -296,7 +330,7 @@
             pltpu.VMEM((5, 8, CH), F32),
             pltpu.VMEM((16, CH), F32),
             pltpu.VMEM((2, 8, CH), F32),
-            pltpu.VMEM((COLS + 16, CH), F32),
+            pltpu.VMEM((4, COLS + 16, CH), F32),
             pltpu.VMEM((2, COLS + 8, CH), F32),
             pltpu.VMEM((FRAMES, BAND + 1, OUT_COLS, 3 * CH), BF16),
             pltpu.VMEM((FRAMES, COLS, CH), BF16),
@@ -309,7 +343,7 @@
             dma((ROWS,)), dma((ROWS,)),
             dma((5,)), dma((5,)),
             dma((2,)), dma((2,)),
-            dma((1,)), dma((1,)),
+            dma((2,)), dma((2,)),
         ],
         compiler_params=pltpu.CompilerParams(
             collective_id=0, has_side_effects=True, vmem_limit_bytes=56 * 1024 * 1024

time: 59.8 us -> 47.9 us (0.80)
  the two profiles are of different devices: /device:TPU:0 before, /device:TPU:1 now
where the time goes in v2:
time: 47.9 us; the launch traced here: 47.8 us
  Pallas kernels  45.9 us (96%)
  local copies, waits for them, and re-layouts  1.89 us (4%)
    pallas_call x1, Pallas kernels, per_device(): pl.pallas_call(kernel, out_shape=jax.ShapeDtypeStruct((FRAMES, OUT_ROWS,...  45.9 us
    unnamed x1, local copies, waits for them, and re-layouts  1.89 us

profile of v2, /device:TPU:1, one launch (start us, length us, event | category | flops | bytes accessed | tf_op | source)
XLA Modules:
  0.0 47.8 jit_solution(16939224922288265429)
XLA Ops:
  0.0 45.9 %encode.1 = bf16[4,4,128,128]{3,2,1,0:T(8,128)(2,1)} custom-call(bf16[4,8,256,128]{3,2,1,0:T(8,128)(2,1)} %video.1, s32[8]{0:T(128)} %clip.1, f32[1,128]{1,0:T(1,128)} %bitcast.4, f32[1,128]{1,0:T(1,128)} %bitcast.5, bf16[3,3,3,128,128]{4,3,2,1,0:T(8,128)(2,1)} %cw_hbm.1, f32[1,128]{1,0:T(1,128)} %bitcast.6, bf16[3,3,3,128,128]{4,3,2,1,0:T(8,128)(2,1)} %dw_hbm.1, ...), custom_call_target="tpu_custom_call" | custom-call | flops 9059999744 | bytes 5000000 | tf_op jit(solution)/shard_map/encode/pallas_call | solution.py:315
  45.9 1.9 %copy.10 = bf16[4,4,128,128]{3,2,1,0:T(8,128)(2,1)} copy(bf16[4,4,128,128]{3,2,1,0:T(8,128)(2,1)} %encode.1) | data formatting | bytes 1048576

commit v3 on v2

--- a/solution.py
+++ b/solution.py
@@ -17,8 +17,8 @@
 
 
 def kernel(
-    video, clip, gain, shift, cw_hbm, cbias, dw_hbm, dbias, out,
-    raw, hid0, hid1, hid2, hid3, hid4, cw, dw, wc, wd, part, tot, rbuf, tbuf, mom, coef, hs, ss, dn,
+    video, clip_hbm, gain_hbm, shift_hbm, cw_hbm, cbias_hbm, dw_hbm, dbias_hbm, out,
+    clip, gain, shift, cbias, dbias, raw, hid0, hid1, hid2, hid3, hid4, cw, dw, wc, wd, part, rbuf, tbuf, mom, coef, hs, ss, dn,
     rowsend, rowrecv, z, psend, precv,
     load_sem, halo_send, halo_recv, r_send, r_recv, t_send, t_recv,
     row_send, row_recv, p_send, p_recv,
@@ -45,6 +45,9 @@
     ]
     loads.append(pltpu.make_async_copy(cw_hbm, cw, load_sem.at[FRAMES]))
     loads.append(pltpu.make_async_copy(dw_hbm, dw, load_sem.at[FRAMES + 1]))
+    small = [(clip_hbm, clip), (gain_hbm, gain), (shift_hbm, shift), (cbias_hbm, cbias), (dbias_hbm, dbias)]
+    for n, (source, target) in enumerate(small):
+        loads.append(pltpu.make_async_copy(source, target, load_sem.at[FRAMES + 2 + n]))
     for copy in loads:
         copy.start()
 
@@ -68,22 +71,29 @@
         part[pl.ds(f, 1)] = jnp.sum(s, axis=0, keepdims=True)
         part[pl.ds(FRAMES + f, 1)] = jnp.sum(q, axis=0, keepdims=True)
 
-    loads[FRAMES].wait()
-    loads[FRAMES + 1].wait()
-
-    def lay_conv(a, carry):
-        for rr in range(4):
-            for e in range(3):
-                at = pl.ds((rr * 3 + e) * CH, CH)
-                empty = jnp.zeros((CH, CH), BF16)
-                wc[a, at, pl.ds(0, CH)] = cw[a, rr, e] if rr < 3 else empty
-                wc[a, at, pl.ds(CH, CH)] = cw[a, rr - 1, e] if rr > 0 else empty
-        return carry
-
-    lax.fori_loop(0, 3, lay_conv, 0)
-    for a in range(3):
-        for be in range(9):
-            wd[pl.ds(be * CH, CH), pl.ds(a * CH, CH)] = dw[a, be // 3, be % 3]
+    pl.semaphore_wait(barrier, len(peers))
+
+    tbuf[2] = part[...]
+    tcopies = [
+        remote(part, tbuf.at[2 - k], t_send.at[2 - k], t_recv.at[2 - k], k, 0)
+        for k in (1, 2, -1, -2)
+    ]
+    for copy in tcopies:
+        copy.start()
+    halos = [
+        remote(video.at[pl.ds(2, 2), pl.ds(4, 4)], raw.at[pl.ds(0, 2), pl.ds(5, 4)], halo_send.at[0], halo_recv.at[0], 1, 0),
+        remote(video.at[:, BAND - 1], raw.at[pl.ds(2, FRAMES), 0], halo_send.at[1], halo_recv.at[1], 0, 1),
+        remote(video.at[pl.ds(0, 2), 0], raw.at[pl.ds(2, 2), BAND + 1], halo_send.at[2], halo_recv.at[2], 0, -1),
+        remote(video.at[pl.ds(2, 2), BAND - 1], raw.at[pl.ds(0, 2), 0], halo_send.at[3], halo_recv.at[3], 1, 1),
+        remote(video.at[pl.ds(2, 2), 0], raw.at[pl.ds(0, 2), BAND + 1], halo_send.at[4], halo_recv.at[4], 1, -1),
+        remote(video.at[pl.ds(2, 2), pl.ds(0, 4)], raw.at[pl.ds(0, 2), pl.ds(1, 4)], halo_send.at[5], halo_recv.at[5], 1, 0),
+        remote(video.at[pl.ds(2, 2), 0], raw.at[pl.ds(4, 2), BAND + 1], halo_send.at[6], halo_recv.at[6], 0, -1),
+    ]
+    halos[2].start()
+    halos[0].start()
+
+    for copy in loads[FRAMES + 2:]:
+        copy.wait()
 
     base = d * FRAMES - 2
     firsts, ends = [], []
@@ -97,45 +107,15 @@
             start = stop
         firsts.append(first - base)
         ends.append(end - base)
-
-    pl.semaphore_wait(barrier, len(peers))
-
-    rcopies = [
-        remote(part, rbuf.at[j], r_send.at[j], r_recv.at[j], 0, j) for j in range(1, ROWS)
-    ]
-    for copy in rcopies:
-        copy.start()
-
-    halos = [
-        remote(video.at[pl.ds(2, 2)], raw.at[pl.ds(0, 2), pl.ds(1, BAND)], halo_send.at[0], halo_recv.at[0], 1, 0),
-        remote(video.at[:, BAND - 1], raw.at[pl.ds(2, FRAMES), 0], halo_send.at[1], halo_recv.at[1], 0, 1),
-        remote(video.at[:, 0], raw.at[pl.ds(2, FRAMES), BAND + 1], halo_send.at[2], halo_recv.at[2], 0, -1),
-        remote(video.at[pl.ds(2, 2), BAND - 1], raw.at[pl.ds(0, 2), 0], halo_send.at[3], halo_recv.at[3], 1, 1),
-        remote(video.at[pl.ds(2, 2), 0], raw.at[pl.ds(0, 2), BAND + 1], halo_send.at[4], halo_recv.at[4], 1, -1),
-    ]
-    for copy in halos:
-        copy.start()
-
-    rbuf[0] = part[...]
-    for copy in rcopies:
-        copy.wait_recv()
-    total = rbuf[0]
-    for j in range(1, ROWS):
-        total = total + rbuf[j]
-    tot[...] = total
-    tbuf[2] = total
-    tcopies = [
-        remote(tot, tbuf.at[2 - k], t_send.at[2 - k], t_recv.at[2 - k], k, 0)
-        for k in (-2, -1, 1, 2)
-    ]
-    for copy in tcopies:
-        copy.start()
+    sub = lax.broadcasted_iota(jnp.int32, (8, CH), 0)
+    count = jnp.ones((8, CH), F32)
+    for e in range(EXT):
+        frames = jnp.maximum(ends[e] - firsts[e], 1)
+        count = jnp.where(sub == e, (frames * (HEIGHT * COLS * PER_GROUP)).astype(F32), count)
+
     for copy in tcopies:
         copy.wait_recv()
-
-    sub = lax.broadcasted_iota(jnp.int32, (8, CH), 0)
     mom[...] = jnp.zeros((16, CH), F32)
-    count = jnp.ones((8, CH), F32)
     for e in range(EXT):
         mine = jnp.zeros((8, CH), F32)
         for k in range(5):
@@ -143,14 +123,40 @@
             mine = mine + jnp.where((at >= firsts[e]) & (at < ends[e]), tbuf[k], 0.0)
         mom[pl.ds(e, 1)] = jnp.sum(jnp.where(sub < FRAMES, mine, 0.0), axis=0, keepdims=True)
         mom[pl.ds(8 + e, 1)] = jnp.sum(jnp.where(sub >= FRAMES, mine, 0.0), axis=0, keepdims=True)
-        frames = jnp.maximum(ends[e] - firsts[e], 1)
-        count = jnp.where(sub == e, (frames * (HEIGHT * COLS * PER_GROUP)).astype(F32), count)
+    rcopies = [
+        remote(mom, rbuf.at[j], r_send.at[j], r_recv.at[j], 0, j) for j in range(1, ROWS)
+    ]
+    for copy in rcopies:
+        copy.start()
+    for j in (6, 1, 4, 5, 3):
+        halos[j].start()
+
+    loads[FRAMES].wait()
+    loads[FRAMES + 1].wait()
+
+    def lay_conv(a, carry):
+        for rr in range(4):
+            for e in range(3):
+                at = pl.ds((rr * 3 + e) * CH, CH)
+                empty = jnp.zeros((CH, CH), BF16)
+                wc[a, at, pl.ds(0, CH)] = cw[a, rr, e] if rr < 3 else empty
+                wc[a, at, pl.ds(CH, CH)] = cw[a, rr - 1, e] if rr > 0 else empty
+        return carry
+
+    lax.fori_loop(0, 3, lay_conv, 0)
+    for a in range(3):
+        for be in range(9):
+            wd[pl.ds(be * CH, CH), pl.ds(a * CH, CH)] = dw[a, be // 3, be % 3]
     lane_a = lax.broadcasted_iota(jnp.int32, (CH, CH), 0) // PER_GROUP
     lane_b = lax.broadcasted_iota(jnp.int32, (CH, CH), 1) // PER_GROUP
     same = jnp.where(lane_a == lane_b, 1.0, 0.0).astype(F32)
-    grouped = jnp.dot(
-        mom[...], same, preferred_element_type=F32, precision=lax.Precision.HIGHEST
-    )
+
+    for copy in rcopies:
+        copy.wait_recv()
+    total = mom[...]
+    for j in range(1, ROWS):
+        total = total + rbuf[j]
+    grouped = jnp.dot(total, same, preferred_element_type=F32, precision=lax.Precision.HIGHEST)
     mean = grouped[0:8] / count
     scale = lax.rsqrt(grouped[8:16] / count - mean * mean + EPSILON)
     slope = scale * gain[...]
@@ -242,6 +248,7 @@
     ]
 
     halos[2].wait_recv()
+    halos[6].wait_recv()
     activate(own, 4)
     activate(own, 3)
     for f in late:
@@ -261,12 +268,13 @@
     partial_sums(OUT_COLS, 3 * OUT_COLS)
     pcopies[0].start()
 
-    for j in (0, 3, 4):
-        halos[j].wait_recv()
+    halos[0].wait_recv()
+    halos[4].wait_recv()
     activate(before, 4)
     activate(before, 3)
     for f in early:
         convolve(f, 3)
+    halos[5].wait_recv()
     activate(before, 2)
     rowcopies[1].start()
     rowcopies[0].wait_recv()
@@ -279,6 +287,7 @@
     activate(before, 1)
     for f in early:
         convolve(f, 1)
+    halos[3].wait_recv()
     activate(before, 0)
     for f in early:
         convolve(f, 0)
@@ -307,17 +316,18 @@
 
 
 def per_device(video, clip_lengths, gain, shift, conv_weight, conv_bias, down_weight, down_bias):
-    any_space = pl.BlockSpec(memory_space=pl.ANY)
+    hbm = pl.BlockSpec(memory_space=pltpu.HBM)
     vmem = pl.BlockSpec(memory_space=pltpu.VMEM)
-    smem = pl.BlockSpec(memory_space=pltpu.SMEM)
     dma = pltpu.SemaphoreType.DMA
     pixels = OUT_ROWS * OUT_COLS
     return pl.pallas_call(
         kernel,
         out_shape=jax.ShapeDtypeStruct((FRAMES, OUT_ROWS, OUT_COLS, CH), BF16),
-        in_specs=[any_space, smem, vmem, vmem, any_space, vmem, any_space, vmem],
+        in_specs=[hbm] * 8,
         out_specs=vmem,
         scratch_shapes=[
+            pltpu.SMEM((8,), jnp.int32),
+            *[pltpu.VMEM((1, CH), F32)] * 4,
             pltpu.VMEM((EXT, BAND + 2, COLS, CH), BF16),
             *[pltpu.VMEM((EXT, 2, COLS, 3 * CH), BF16)] * 5,
             pltpu.VMEM((3, 3, 3, CH, CH), BF16),
@@ -325,8 +335,7 @@
             pltpu.VMEM((3, 12 * CH, 2 * CH), BF16),
             pltpu.VMEM((9 * CH, 3 * CH), BF16),
             pltpu.VMEM((8, CH), F32),
-            pltpu.VMEM((8, CH), F32),
-            pltpu.VMEM((ROWS, 8, CH), F32),
+            pltpu.VMEM((ROWS, 16, CH), F32),
             pltpu.VMEM((5, 8, CH), F32),
             pltpu.VMEM((16, CH), F32),
             pltpu.VMEM((2, 8, CH), F32),
@@ -338,8 +347,8 @@
             pltpu.VMEM((FRAMES, pixels, 3 * CH), F32),
             pltpu.VMEM((2, pixels, CH), F32),
             pltpu.VMEM((2, pixels, CH), F32),
-            dma((FRAMES + 2,)),
-            dma((5,)), dma((5,)),
+            dma((FRAMES + 7,)),
+            dma((7,)), dma((7,)),
             dma((ROWS,)), dma((ROWS,)),
             dma((5,)), dma((5,)),
             dma((2,)), dma((2,)),

time: 47.9 us -> 40.1 us (0.84)
  the two profiles are of different devices: /device:TPU:1 before, /device:TPU:0 now
where the time goes in v3:
time: 40.1 us; the launch traced here: 40 us
  Pallas kernels  38.1 us (95%)
  local copies, waits for them, and re-layouts  1.89 us (5%)
    pallas_call x1, Pallas kernels, per_device(): pl.pallas_call(kernel, out_shape=jax.ShapeDtypeStruct((FRAMES, OUT_ROWS,...  38.1 us
    unnamed x1, local copies, waits for them, and re-layouts  1.89 us

profile of v3, /device:TPU:0, one launch (start us, length us, event | category | flops | bytes accessed | tf_op | source)
XLA Modules:
  0.0 40.0 jit_solution(8568395476896344791)
XLA Ops:
  0.0 38.1 %encode.1 = bf16[4,4,128,128]{3,2,1,0:T(8,128)(2,1)} custom-call(bf16[4,8,256,128]{3,2,1,0:T(8,128)(2,1)} %video.1, s32[8]{0:T(128)} %clip_hbm.1, f32[1,128]{1,0:T(1,128)} %bitcast.4, f32[1,128]{1,0:T(1,128)} %bitcast.5, bf16[3,3,3,128,128]{4,3,2,1,0:T(8,128)(2,1)} %cw_hbm.1, f32[1,128]{1,0:T(1,128)} %bitcast.6, bf16[3,3,3,128,128]{4,3,2,1,0:T(8,128)(2,1)} %dw_hbm.1, ...), custom_call_target="tpu_custom_call" | custom-call | flops 9059999744 | bytes 5000000 | tf_op jit(solution)/shard_map/encode/pallas_call | solution.py:323
  38.1 1.9 %copy.10 = bf16[4,4,128,128]{3,2,1,0:T(8,128)(2,1)} copy(bf16[4,4,128,128]{3,2,1,0:T(8,128)(2,1)} %encode.1) | data formatting | bytes 1048576

commit v4 on v3

--- a/solution.py
+++ b/solution.py
@@ -247,44 +247,44 @@
         remote(psend.at[:, top], precv.at[:, top], p_send.at[1], p_recv.at[1], 1, 0),
     ]
 
-    halos[2].wait_recv()
-    halos[6].wait_recv()
-    activate(own, 4)
     activate(own, 3)
-    for f in late:
-        convolve(f, 3)
     activate(own, 2)
-    rowcopies[0].start()
     for f in late:
         convolve(f, 2)
     activate(own, 1)
+    halos[2].wait_recv()
+    halos[6].wait_recv()
+    for f in late:
+        convolve(f, 1)
+    activate(own, 4)
     halos[1].wait_recv()
     for f in late:
-        convolve(f, 1)
+        convolve(f, 3)
     activate(own, 0)
+    rowcopies[0].start()
+    halos[0].wait_recv()
+    halos[4].wait_recv()
     for f in late:
         convolve(f, 0)
+    activate(before, 4)
+    activate(before, 3)
     downsample((2, 3), (1, 2, 3))
     partial_sums(OUT_COLS, 3 * OUT_COLS)
     pcopies[0].start()
 
-    halos[0].wait_recv()
-    halos[4].wait_recv()
-    activate(before, 4)
-    activate(before, 3)
     for f in early:
         convolve(f, 3)
     halos[5].wait_recv()
     activate(before, 2)
     rowcopies[1].start()
+    for f in early:
+        convolve(f, 2)
+    activate(before, 1)
     rowcopies[0].wait_recv()
     upper(late)
     downsample((2, 3), (0,))
     partial_sums(0, OUT_COLS)
     pcopies[1].start()
-    for f in early:
-        convolve(f, 2)
-    activate(before, 1)
     for f in early:
         convolve(f, 1)
     halos[3].wait_recv()

time: 40.1 us -> 38.9 us (0.970)
  Pallas kernels: 38.1 us -> 36.9 us
    pallas_call x1, Pallas kernels: 38.1 us -> 36.9 us  [per_device(): pl.pallas_call(kernel, out_shape=jax.ShapeDtypeStruct((FRAMES, OUT_ROWS,...]
where the time goes in v4:
time: 38.9 us; the launch traced here: 38.8 us
  Pallas kernels  36.9 us (95%)
  local copies, waits for them, and re-layouts  1.89 us (5%)
    pallas_call x1, Pallas kernels, per_device(): pl.pallas_call(kernel, out_shape=jax.ShapeDtypeStruct((FRAMES, OUT_ROWS,...  36.9 us
    unnamed x1, local copies, waits for them, and re-layouts  1.89 us

profile of v4, /device:TPU:0, one launch (start us, length us, event | category | flops | bytes accessed | tf_op | source)
XLA Modules:
  0.0 38.8 jit_solution(13795128971669724214)
XLA Ops:
  0.0 36.9 %encode.1 = bf16[4,4,128,128]{3,2,1,0:T(8,128)(2,1)} custom-call(bf16[4,8,256,128]{3,2,1,0:T(8,128)(2,1)} %video.1, s32[8]{0:T(128)} %clip_hbm.1, f32[1,128]{1,0:T(1,128)} %bitcast.4, f32[1,128]{1,0:T(1,128)} %bitcast.5, bf16[3,3,3,128,128]{4,3,2,1,0:T(8,128)(2,1)} %cw_hbm.1, f32[1,128]{1,0:T(1,128)} %bitcast.6, bf16[3,3,3,128,128]{4,3,2,1,0:T(8,128)(2,1)} %dw_hbm.1, ...), custom_call_target="tpu_custom_call" | custom-call | flops 9059999744 | bytes 5000000 | tf_op jit(solution)/shard_map/encode/pallas_call | solution.py:323
  36.9 1.9 %copy.10 = bf16[4,4,128,128]{3,2,1,0:T(8,128)(2,1)} copy(bf16[4,4,128,128]{3,2,1,0:T(8,128)(2,1)} %encode.1) | data formatting | bytes 1048576

commit v5 on v4

--- a/solution.py
+++ b/solution.py
@@ -48,7 +48,7 @@
     small = [(clip_hbm, clip), (gain_hbm, gain), (shift_hbm, shift), (cbias_hbm, cbias), (dbias_hbm, dbias)]
     for n, (source, target) in enumerate(small):
         loads.append(pltpu.make_async_copy(source, target, load_sem.at[FRAMES + 2 + n]))
-    for copy in loads:
+    for copy in loads[:FRAMES] + loads[FRAMES + 2:]:
         copy.start()
 
     barrier = pltpu.get_barrier_semaphore()
@@ -71,6 +71,8 @@
         part[pl.ds(f, 1)] = jnp.sum(s, axis=0, keepdims=True)
         part[pl.ds(FRAMES + f, 1)] = jnp.sum(q, axis=0, keepdims=True)
 
+    for copy in loads[FRAMES:FRAMES + 2]:
+        copy.start()
     pl.semaphore_wait(barrier, len(peers))
 
     tbuf[2] = part[...]

time: 38.9 us -> 38.9 us (level)
  no operation moved by 1% of the time
where the time goes in v5:
time: 38.9 us; the launch traced here: 38.8 us
  Pallas kernels  36.9 us (95%)
  local copies, waits for them, and re-layouts  1.89 us (5%)
    pallas_call x1, Pallas kernels, per_device(): pl.pallas_call(kernel, out_shape=jax.ShapeDtypeStruct((FRAMES, OUT_ROWS,...  36.9 us
    unnamed x1, local copies, waits for them, and re-layouts  1.89 us

profile of v5, /device:TPU:0, one launch (start us, length us, event | category | flops | bytes accessed | tf_op | source)
XLA Modules:
  0.0 38.8 jit_solution(8078089098249943278)
XLA Ops:
  0.0 36.9 %encode.1 = bf16[4,4,128,128]{3,2,1,0:T(8,128)(2,1)} custom-call(bf16[4,8,256,128]{3,2,1,0:T(8,128)(2,1)} %video.1, s32[8]{0:T(128)} %clip_hbm.1, f32[1,128]{1,0:T(1,128)} %bitcast.4, f32[1,128]{1,0:T(1,128)} %bitcast.5, bf16[3,3,3,128,128]{4,3,2,1,0:T(8,128)(2,1)} %cw_hbm.1, f32[1,128]{1,0:T(1,128)} %bitcast.6, bf16[3,3,3,128,128]{4,3,2,1,0:T(8,128)(2,1)} %dw_hbm.1, ...), custom_call_target="tpu_custom_call" | custom-call | flops 9059999744 | bytes 5000000 | tf_op jit(solution)/shard_map/encode/pallas_call | solution.py:325
  36.9 1.9 %copy.10 = bf16[4,4,128,128]{3,2,1,0:T(8,128)(2,1)} copy(bf16[4,4,128,128]{3,2,1,0:T(8,128)(2,1)} %encode.1) | data formatting | bytes 1048576
